TPU v7x, 32 devices: a whole 2x2x4 slice. The times are simulated.
32 devices in a mesh: order: 4 (over y, x), lat: 8 (over z, core).
Axes of the slice: x: 2, y: 2, z: 4, core: 2. Of those that a mesh axis runs over, the one named last changes fastest.
Arguments:
- fourier: bfloat16 [128, 64, 2048], P('order', None, 'lat'), may hold values from -6 to 6
- quad_weights: float32 [2048], P('lat'), may hold values from 0.5 to 1.5
- leaf_basis: bfloat16 [128, 64, 2048], P('order', None, 'lat'), may hold values from -0.375 to 0.375
- level_factors: bfloat16 [128, 3, 2, 8, 64, 64], P('order', None, None, 'lat'), may hold values from -0.5 to 0.5
- sparsity: int32 [128, 3, 8], P('order', None, 'lat'), may hold values 0 or 1
- root_basis: bfloat16 [128, 64, 2048], P(None, None, 'lat'), may hold values from -0.75 to 0.75
- order_of_slot: int32 [128], replicated, may hold values from 0 to 127, each once
Outputs:
- spectra: bfloat16 [32, 2, 2048, 128], P('order', None, 'lat')
Inputs may be any that keep to these rules, and one draw needn't show every extreme that they name: `order_of_slot`: every window index appears in exactly one slot.
All inputs are finite; a program needn't handle non-finite values. No bound on the sum of `sparsity` on one device may be relied on, other than what follows from the above.
Results may differ from a plain program's by a relative error of at most 0.0081.
Values may be sent and summed in bfloat16 or wider, within the bound.
No kernel may reach another device: no remote copies, remote signals or barrier semaphores. Data moves between devices by JAX's collectives and lax.ppermute only.
A program may use at most 64 MiB of HBM per device.

v0:
```python
import functools

import jax
import jax.numpy as jnp
from jax import lax
from jax.experimental import pallas as pl
from jax.experimental.pallas import tpu as pltpu
from jax.sharding import PartitionSpec as P

DEGREES = 2048
F32, BF16 = jnp.float32, jnp.bfloat16
MIB = 1 << 20
IN_HBM = pl.BlockSpec(memory_space=pltpu.HBM)
IN_SMEM = pl.BlockSpec(memory_space=pltpu.SMEM)
ANYWHERE = pl.BlockSpec(memory_space=pl.ANY)


def contract(lhs, rhs, dims):
    return lax.dot_general(lhs, rhs, (dims, ((), ())), preferred_element_type=F32)


def in_hbm(array):
    return pltpu.with_memory_space_constraint(array, pltpu.HBM)


def call(kernel, name, out_shape, in_specs, flops, size, scratch=(), mib=16, **more):
    return pl.pallas_call(
        kernel,
        out_shape=out_shape,
        in_specs=in_specs,
        scratch_shapes=list(scratch),
        compiler_params=pltpu.CompilerParams(vmem_limit_bytes=mib * MIB),
        cost_estimate=pl.CostEstimate(flops=flops // 1000, bytes_accessed=size // 1000, transcendentals=0),
        name=name,
        **more,
    )


def whole_blocks(count):
    return [pl.BlockSpec()] * count


def leaf_kernel(
    pieces, group, fourier_hbm, weight_hbm, leaf_hbm, state_ref, fourier_ref, weight_ref, leaf_ref, sems
):
    side = lax.axis_index("order") & 1
    slots, columns, lats = fourier_ref.shape
    rank = leaf_ref.shape[1]
    per = slots // pieces
    copies = [pltpu.make_async_copy(weight_hbm, weight_ref, sems.at[0])]
    for piece in range(pieces):
        part = pl.ds(piece * per, per)
        copies.append(pltpu.make_async_copy(fourier_hbm.at[part], fourier_ref.at[part], sems.at[1 + 2 * piece]))
        copies.append(pltpu.make_async_copy(leaf_hbm.at[part], leaf_ref.at[part], sems.at[2 + 2 * piece]))
    for copy in copies:
        copy.start()
    copies[0].wait()
    weight = weight_ref[...]
    mine = lax.broadcasted_iota(jnp.int32, (columns, 2 * rank), 1) < rank
    for pair in range(slots // 2):
        if 2 * pair % per == 0:
            copies[1 + 2 * (2 * pair // per)].wait()
            copies[2 + 2 * (2 * pair // per)].wait()
        both = pl.ds(2 * pair, 2)
        weighted = (fourier_ref[both].astype(F32) * weight[None]).astype(BF16)
        product = contract(
            weighted.reshape(2 * columns, lats), leaf_ref[both].reshape(2 * rank, lats), ((1,), (1,))
        )
        state = jnp.where(mine, product[:columns], product[columns:]).astype(BF16)
        if group % 16:
            state_ref[pair] = state
            continue
        for owner in range(columns // group):
            rows = pl.ds(owner // 2 * group, group)
            state_ref[pair, owner % 2 ^ side, rows] = state[owner * group : (owner + 1) * group]


def leaf_states(fourier, quad_weights, leaf_basis, owners):
    slots, columns, lats = fourier.shape
    rank = leaf_basis.shape[1]
    pairs, half, lanes, group = slots // 2, columns // 2, 2 * rank, columns // owners
    pieces = 2
    state = call(
        functools.partial(leaf_kernel, pieces, group),
        "leaf",
        jax.ShapeDtypeStruct((pairs, columns, lanes) if group % 16 else (pairs, 2, half, lanes), BF16),
        [IN_HBM] * 3,
        2 * slots * columns * rank * lats,
        4 * slots * columns * lats,
        [
            pltpu.VMEM((slots, columns, lats), BF16),
            pltpu.VMEM((1, lats), F32),
            pltpu.VMEM((slots, rank, lats), BF16),
            pltpu.SemaphoreType.DMA((1 + 2 * pieces,)),
        ],
    )(fourier, quad_weights, leaf_basis)
    if group % 16:
        side = lax.axis_index("order") & 1
        state = state.reshape(pairs, owners // 2, 2, group, lanes)
        sides = [lax.dynamic_index_in_dim(state, side ^ i, 2, False).reshape(pairs, half, lanes) for i in range(2)]
        state = jnp.stack(sides, axis=1)
    return state


def factor_kernel(levels, pieces, factor_hbm, present_hbm, after, *refs):
    del after
    weight_refs, (factor_ref, present_ref, sems) = refs[:-3], refs[-3:]
    present_copy = pltpu.make_async_copy(present_hbm, present_ref, sems.at[len(levels) * pieces])
    present_copy.start()
    _, slots, _, rank, _ = factor_ref.shape
    per = slots // pieces
    copies = {}
    for i, level in enumerate(levels):
        for piece in range(pieces):
            part = pl.ds(piece * per, per)
            copies[i, piece] = pltpu.make_async_copy(
                factor_hbm.at[part, level, :, 0], factor_ref.at[i, part], sems.at[i * pieces + piece]
            )
            copies[i, piece].start()
    empty = jnp.zeros((rank, rank), BF16)
    present_copy.wait()
    for i, level in enumerate(levels):
        for pair in range(slots // 2):
            if 2 * pair % per == 0:
                copies[i, 2 * pair // per].wait()
            for half in range(2):
                first, second = (factor_ref[i, slot, half] for slot in (2 * pair, 2 * pair + 1))
                if half:
                    first = jnp.where(present_ref[level, 0, 2 * pair] != 0, first, empty)
                    second = jnp.where(present_ref[level, 0, 2 * pair + 1] != 0, second, empty)
                if weight_refs[i].shape[1] == rank:
                    weight_refs[i + half][pair] = jnp.concatenate([first, second], axis=1)
                    continue
                lanes = pl.ds(half * 2 * rank, 2 * rank)
                weight_refs[i][pair, :rank, lanes] = jnp.concatenate([first, empty], axis=1)
                weight_refs[i][pair, rank:, lanes] = jnp.concatenate([empty, second], axis=1)


def level_weights(level_factors, present, levels, after):
    slots, last, _, _, rank, _ = level_factors.shape
    count, pieces = len(levels), 2
    return call(
        functools.partial(factor_kernel, levels, pieces),
        "factors",
        [
            jax.ShapeDtypeStruct((slots // 2, *((rank, 2 * rank) if level == last - 1 else (2 * rank, 4 * rank))), BF16)
            for level in levels
            for _ in range(1 + (level == last - 1))
        ],
        [IN_HBM, IN_HBM, ANYWHERE],
        slots * rank * rank * 4 * count,
        slots * rank * rank * 16 * count,
        [
            pltpu.VMEM((count, slots, 2, rank, rank), BF16),
            pltpu.SMEM(present.shape, jnp.int32),
            pltpu.SemaphoreType.DMA((count * pieces + 1,)),
        ],
        mib=24,
    )(level_factors, present, after)


def level_kernel(side, state_ref, partner_ref, weight_ref, out_ref):
    for pair in range(out_ref.shape[0]):
        at = pair if side is None else (pair, side)
        both = jnp.concatenate([state_ref[at], partner_ref[at]], axis=1)
        out_ref[pair] = contract(both, weight_ref[pair], ((1,), (1,))).astype(BF16)


def next_states(name, state, partner, weights, side=None):
    pairs, rows, lanes = state.shape[0], *state.shape[-2:]
    return call(
        functools.partial(level_kernel, side),
        name,
        jax.ShapeDtypeStruct((pairs, rows, lanes), BF16),
        whole_blocks(3),
        4 * pairs * rows * lanes * lanes,
        6 * pairs * rows * lanes,
    )(state, partner, weights)


def by_slot(packed):
    first = lax.broadcasted_iota(jnp.int32, packed.shape, 1) < packed.shape[0]
    empty = jnp.zeros(packed.shape, BF16)
    return jnp.concatenate([jnp.where(first, packed, empty), jnp.where(first, empty, packed)], axis=0)


def own_term_kernel(after, state_ref, own_ref, out_ref):
    del after
    for pair in range(state_ref.shape[0]):
        out_ref[pair] = contract(state_ref[pair], by_slot(own_ref[pair]), ((1,), (1,))).astype(BF16)


def own_term(after, state, own):
    pairs, rows, lanes = state.shape
    return call(
        own_term_kernel,
        "own_term",
        jax.ShapeDtypeStruct(state.shape, BF16),
        [ANYWHERE] + whole_blocks(2),
        2 * pairs * rows * lanes * lanes,
        6 * pairs * rows * lanes,
    )(after, state, own)


def last_level_kernel(axis, after, own_ref, partner_ref, cross_ref, *refs):
    del after
    refs = list(refs)
    own_factor_ref = refs.pop(0) if refs[0].shape == cross_ref.shape else None
    out_refs, groups_ref = refs[:-1], refs[-1]
    me = lax.axis_index(axis) // 2
    pairs, owners, group, _ = groups_ref.shape
    for pair in range(pairs):
        cross = by_slot(cross_ref[pair])
        if own_factor_ref is None:
            result = own_ref[pair].astype(F32) + contract(partner_ref[pair], cross, ((1,), (1,)))
        else:
            weight = jnp.concatenate([by_slot(own_factor_ref[pair]), cross], axis=1)
            both = jnp.concatenate([own_ref[pair], partner_ref[pair]], axis=1)
            result = contract(both, weight, ((1,), (1,)))
        result = result.astype(BF16)
        if len(out_refs) == 1:
            out_refs[0][pair] = result
            continue
        for owner in range(owners):
            groups_ref[pair, owner] = result[owner * group : (owner + 1) * group]
    if len(out_refs) > 1:
        for k, out_ref in enumerate(out_refs):
            for pair in range(pairs):
                out_ref[pl.ds(pair * group, group)] = groups_ref[pair, me ^ k]


def last_states(name, after, own, partner, factors, owners):
    pairs, columns, lanes = own.shape
    group = columns // owners
    rows = pairs * group
    by_owner = group % 16 == 0 and owners > 1
    parts = call(
        functools.partial(last_level_kernel, "order"),
        name,
        [jax.ShapeDtypeStruct((rows, lanes), BF16)] * owners if by_owner else [jax.ShapeDtypeStruct(own.shape, BF16)],
        [ANYWHERE] + whole_blocks(2 + len(factors)),
        4 * pairs * columns * lanes * lanes,
        6 * pairs * columns * lanes,
        [pltpu.VMEM((pairs, owners, group, lanes), BF16)],
    )(after, own, partner, *factors)
    if by_owner:
        return parts
    me = lax.axis_index("order") // 2
    parts = [lax.dynamic_slice_in_dim(parts[0], (me ^ k) * group, group, 1) for k in range(owners)]
    return [part.reshape(rows, lanes) for part in parts]


def near_kernel(group, root_hbm, order_ref, after, root_ref, place_ref, alive_ref, rows_ref, sems):
    del after
    owners, here, _, degrees = root_ref.shape
    slots = rows_ref.shape[1]
    me = lax.axis_index("order")
    copies = []
    for k in range(owners):
        copies.append(pltpu.make_async_copy(root_hbm.at[pl.ds((me ^ k) * here, here)], root_ref.at[k], sems.at[k]))
        copies[-1].start()
    lane = lax.broadcasted_iota(jnp.int32, (1, slots), 1)
    for k in range(owners):
        for slot in range(here):
            pair, half = slot // 2, slot % 2
            row = (pair // group * 2 + half) * group + pair % group
            rows_ref[pl.ds(row, 1), :] = (lane == order_ref[(me ^ k) * here + slot]).astype(F32)
        place_ref[k] = rows_ref[...].astype(BF16)
    degree = lax.axis_index("lat") * degrees + lax.broadcasted_iota(jnp.int32, (degrees, slots), 0)
    window = DEGREES // slots * lax.broadcasted_iota(jnp.int32, (degrees, slots), 1)
    alive_ref[...] = (degree >= window).astype(F32).astype(BF16)
    for copy in copies:
        copy.wait()


def near_roots(root_basis, order_of_slot, owners, group, after):
    slots, rank, degrees = root_basis.shape
    here = slots // owners
    return call(
        functools.partial(near_kernel, group),
        "near_roots",
        [
            jax.ShapeDtypeStruct((owners, here, rank, degrees), BF16),
            jax.ShapeDtypeStruct((owners, here, slots), BF16),
            jax.ShapeDtypeStruct((degrees, slots), BF16),
        ],
        [IN_HBM, IN_SMEM, ANYWHERE],
        slots * slots,
        4 * slots * rank * degrees,
        [pltpu.VMEM((here, slots), F32), pltpu.SemaphoreType.DMA((owners,))],
    )(root_basis, order_of_slot, after)


def root_kernel(group, first, last, *refs):
    refs = list(refs)
    so_far_ref = refs.pop(0) if last else None
    root_ref, place_ref, alive_ref = refs[:3]
    count = len(refs) - (7 if last else 5)
    state_refs = refs[3 : 3 + count]
    out_ref, rows_ref = refs[3 + count : 5 + count]
    natural_ref = refs[5 + count] if last else out_ref
    fields, parts, degrees, slots = out_ref.shape
    columns = fields * parts
    rank = root_ref.shape[2]
    group_rows = group * columns
    here = place_ref.shape[1]
    steps = state_refs[0].shape[0] // group_rows
    shape = (group_rows, 2 * rank)
    row_pair = lax.broadcasted_iota(jnp.int32, shape, 0) // columns
    row_half = lax.broadcasted_iota(jnp.int32, shape, 1) // rank
    masks = [[(row_pair == pair) & (row_half == half) for pair in range(group)] for half in range(2)]
    empty = jnp.zeros(shape, BF16)
    for i, state_ref in enumerate(state_refs):
        for step in range(steps):
            state = state_ref[pl.ds(step * group_rows, group_rows)]
            left = jnp.concatenate(
                [jnp.concatenate([jnp.where(m, state, empty) for m in line], axis=1) for line in masks], axis=0
            )
            right = root_ref[first + i, pl.ds(step * group * 2, group * 2)].reshape(group * 2 * rank, degrees)
            product = contract(left, right, ((1,), (0,)))
            begin = (i * steps + step) * 2 * group_rows
            for tile in range(degrees // 128):
                rows_ref[tile, pl.ds(begin, 2 * group_rows), :] = product[:, tile * 128 : (tile + 1) * 128]
    place = place_ref[pl.ds(first, count)].reshape(count * here, slots)
    copies = []
    for column in range(columns):
        for tile in range(degrees // 128):
            span = slice(tile * 128, (tile + 1) * 128)
            one = rows_ref[tile, pl.ds(column, count * here, stride=columns), :].astype(BF16)
            natural = contract(one.T, place, ((1,), (0,))).astype(BF16)
            where = (column // 2, column % 2, span)
            if last:
                natural = natural + so_far_ref[where]
                natural = jnp.where(alive_ref[span] != 0, natural, jnp.zeros((), BF16))
            natural_ref[where] = natural
        if last:
            where = (column // 2, column % 2)
            copies.append(pltpu.make_async_copy(natural_ref.at[where], out_ref.at[where], refs[-1].at[column]))
            copies[-1].start()
    for copy in copies:
        copy.wait()


def spectra_of(states, roots, places, alive, so_far, first, group):
    state_rows, lanes = states[0].shape
    owners, here, rank, degrees = roots.shape
    slots = places.shape[2]
    columns = state_rows * 2 // here
    last = so_far is not None
    shape = (columns // 2, 2, degrees, slots)
    inputs = ([so_far] if last else []) + [roots, places, alive, *states]
    scratch = [pltpu.VMEM((degrees // 128, len(states) * here * columns, 128), F32)]
    more = {}
    if last:
        scratch += [pltpu.VMEM(shape, BF16), pltpu.SemaphoreType.DMA((columns,))]
        more["out_specs"] = IN_HBM
    return call(
        functools.partial(root_kernel, group, first, last),
        "root",
        jax.ShapeDtypeStruct(shape, BF16),
        whole_blocks(len(inputs)),
        2 * len(states) * here * rank * degrees * columns,
        2 * len(states) * here * rank * degrees,
        scratch,
        mib=24,
        **more,
    )(*inputs)


def per_device(
    fourier, quad_weights, leaf_basis, level_factors, sparsity, root_basis, order_of_slot
):
    slots, columns, lats = fourier.shape
    owners = lax.axis_size("order")
    levels = level_factors.shape[1]
    group = max(2, 16 * owners // columns)
    present = in_hbm(sparsity.transpose(1, 2, 0))
    fourier, leaf_basis, level_factors, root_basis = map(in_hbm, (fourier, leaf_basis, level_factors, root_basis))
    quad_weights = in_hbm(quad_weights.reshape(1, lats))

    def swap(array, axis, bits):
        return lax.ppermute(array, axis, [(i, i ^ bits) for i in range(lax.axis_size(axis))])

    def swap_both(array, order_bits, lat_bits):
        blocks = lax.axis_size("lat")
        pairs = [
            (o * blocks + b, (o ^ order_bits) * blocks + (b ^ lat_bits)) for o in range(owners) for b in range(blocks)
        ]
        return lax.ppermute(array, ("order", "lat"), pairs)

    state = leaf_states(fourier, quad_weights, leaf_basis, owners)
    partner = swap(state, "lat", 1)
    weights = level_weights(level_factors, present, (0,), state)
    states = [next_states(f"level0_{c}", state, partner, weights[0], c) for c in range(2)]
    weights += level_weights(level_factors, present, tuple(range(1, levels)), states[1])
    own_factors, cross_factors = weights[-2:]
    other_cross = swap(cross_factors, "order", 1)
    for level in range(1, levels - 1):
        partners = [swap(state, "lat", 1 << level) for state in states]
        states = [next_states(f"level{level}_{c}", states[c], partners[c], weights[level]) for c in range(2)]
    top = 1 << levels - 1
    partner = swap(states[0], "lat", top)
    other_partner = swap_both(states[1], 1, top)
    other_own = swap(own_term(states[1], states[1], own_factors), "order", 1)
    roots, places, alive = near_roots(root_basis, order_of_slot, owners, group, states[1])
    both = (
        last_states("last_own", alive, states[0], partner, (cross_factors, own_factors), owners // 2),
        last_states("last_other", alive, other_own, other_partner, (other_cross,), owners // 2),
    )
    arrived = [swap(both[k % 2][k // 2], "order", k // 2 * 2) if k > 1 else both[k][0] for k in range(owners)]
    early = 3 * owners // 4
    spectra = spectra_of(arrived[:early], roots, places, alive, None, 0, group)
    return spectra_of(arrived[early:], roots, places, alive, spectra, early, group)


def solution(mesh):
    return jax.shard_map(
        per_device,
        mesh=mesh,
        in_specs=(
            P("order", None, "lat"),
            P("lat"),
            P("order", None, "lat"),
            P("order", None, None, "lat", None, None),
            P("order", None, "lat"),
            P(None, None, "lat"),
            P(),
        ),
        out_specs=P("order", None, "lat", None),
        check_vma=False,
    )
```

profile of v0, /device:TPU:0, one launch (start us, length us, event | category | flops | bytes accessed | tf_op | source)
XLA Modules:
  0.0 33.5 jit_solution(8641157967166814153)
XLA Ops:
  0.0 1.9 %leaf.1.after.state_ref = bf16[16,2,32,128]{3,2,1,0:T(8,128)(2,1)S(1)} custom-call(bf16[32,64,256]{2,1,0:T(8,128)(2,1)} %fourier_hbm.1, f32[1,256]{1,0:T(1,128)} %bitcast.4, bf16[32,64,256]{2,1,0:T(8,128)(2,1)} %leaf_hbm.1), custom_call_target="tpu_custom_call" | custom-call | flops 67108 | bytes 2097 | tf_op jit(solution)/shard_map/leaf/pallas_call | solution.py:83
  1.9 0.5 %collective-permute-start = (bf16[16,2,32,128]{3,2,1,0:T(8,128)(2,1)S(1)}, bf16[16,2,32,128]{3,2,1,0:T(8,128)(2,1)S(1)}, u32[]{:S(2)}, u32[]{:S(2)}) collective-permute-start(bf16[16,2,32,128]{3,2,1,0:T(8,128)(2,1)S(1)} %leaf.1.after.state_ref), channel_id=1, source_target_pairs={{0,1},{1,0},{2,3},{3,2},{4,5},{5,4},{6,7},{7,6},{8,9},{9,8},{10,11... | collective-permute-start | bytes 786440 | tf_op jit(solution)/shard_map/ppermute | solution.py:382
  2.4 1.4 %factors.2.weight_ref = bf16[16,128,256]{2,1,0:T(8,128)(2,1)S(1)} custom-call(bf16[32,3,2,1,64,64]{5,4,3,2,1,0:T(8,128)(2,1)} %factor_hbm.3, s32[3,1,32]{2,1,0:T(1,128)} %bitcast.2, bf16[16,2,32,128]{3,2,1,0:T(8,128)(2,1)S(1)} %leaf.1.after.state_ref), custom_call_target="tpu_custom_call" | custom-call | flops 524 | bytes 2097 | tf_op jit(solution)/shard_map/factors/pallas_call | solution.py:142
  3.9 0.0 collective-permute-done.partner_ref
  3.9 0.4 %level0_0.1.state_ref = bf16[16,32,128]{2,1,0:T(8,128)(2,1)S(1)} custom-call(bf16[16,2,32,128]{3,2,1,0:T(8,128)(2,1)S(1)} %leaf.1.after.state_ref, bf16[16,2,32,128]{3,2,1,0:T(8,128)(2,1)S(1)} %collective-permute-done.partner_ref, bf16[16,128,256]{2,1,0:T(8,128)(2,1)S(1)} %factors.2.weight_ref), custom_call_target="tpu_custom_call" | custom-call | flops 33554 | bytes 393 | tf_op jit(solution)/shard_map/level0_0/pallas_call | solution.py:171
  4.3 0.0 copy-start
  4.3 2.7 %collective-permute-start.2 = (bf16[16,32,128]{2,1,0:T(8,128)(2,1)S(1)}, bf16[16,32,128]{2,1,0:T(8,128)(2,1)S(1)}, u32[]{:S(2)}, u32[]{:S(2)}) collective-permute-start(bf16[16,32,128]{2,1,0:T(8,128)(2,1)S(1)} %level0_0.1.state_ref), channel_id=1, source_target_pairs={{0,2},{1,3},{2,0},{3,1},{4,6},{5,7},{6,4},{7,5},{8,10},{9,11},{10,... | collective-permute-start | bytes 393224 | tf_op jit(solution)/shard_map/ppermute | solution.py:382
  7.0 0.4 %level0_1.1.after.state_ref = bf16[16,32,128]{2,1,0:T(8,128)(2,1)S(1)} custom-call(bf16[16,2,32,128]{3,2,1,0:T(8,128)(2,1)S(1)} %leaf.1.after.state_ref, bf16[16,2,32,128]{3,2,1,0:T(8,128)(2,1)S(1)} %collective-permute-done.partner_ref, bf16[16,128,256]{2,1,0:T(8,128)(2,1)S(1)} %factors.2.weight_ref), custom_call_target="tpu_custom_call" | custom-call | flops 33554 | bytes 393 | tf_op jit(solution)/shard_map/level0_1/pallas_call | solution.py:171
  7.5 0.1 collective-permute-start.1
  7.5 1.7 %factors.3 = (bf16[16,128,256]{2,1,0:T(8,128)(2,1)S(1)}, bf16[16,64,128]{2,1,0:T(8,128)(2,1)S(1)}, bf16[16,64,128]{2,1,0:T(8,128)(2,1)S(1)}) custom-call(bf16[32,3,2,1,64,64]{5,4,3,2,1,0:T(8,128)(2,1)} %factor_hbm.3, s32[3,1,32]{2,1,0:T(1,128)} %bitcast.3, bf16[16,32,128]{2,1,0:T(8,128)(2,1)S(1)} %level0_1.1.after.state_ref), custom_call_target="tpu_custom_call" | custom-call | flops 1048 | bytes 4194 | tf_op jit(solution)/shard_map/factors/pallas_call | solution.py:142
  9.3 2.0 %collective-permute-start.6 = (bf16[16,64,128]{2,1,0:T(8,128)(2,1)S(1)}, bf16[16,64,128]{2,1,0:T(8,128)(2,1)S(1)}, u32[]{:S(2)}, u32[]{:S(2)}) collective-permute-start(bf16[16,64,128]{2,1,0:T(8,128)(2,1)S(1)} %get-tuple-element.19.cross_ref), channel_id=1, source_target_pairs={{0,8},{8,0},{16,24},{24,16},{1,9},{9,1},{17,25},{25,17},{2,10},{10... | collective-permute-start | bytes 786440 | tf_op jit(solution)/shard_map/ppermute | solution.py:382
  11.3 0.1 collective-permute-done.2.partner_ref
  11.4 0.4 %level1_0.1.own_ref = bf16[16,32,128]{2,1,0:T(8,128)(2,1)S(1)} custom-call(bf16[16,32,128]{2,1,0:T(8,128)(2,1)S(1)} %level0_0.1.state_ref, bf16[16,32,128]{2,1,0:T(8,128)(2,1)S(1)} %collective-permute-done.2.partner_ref, bf16[16,128,256]{2,1,0:T(8,128)(2,1)S(1)} %get-tuple-element.15.weight_ref), custom_call_target="tpu_custom_call" | custom-call | flops 33554 | bytes 393 | tf_op jit(solution)/shard_map/level1_0/pallas_call | solution.py:171
  11.8 3.0 %collective-permute-start.3 = (bf16[16,32,128]{2,1,0:T(8,128)(2,1)S(1)}, bf16[16,32,128]{2,1,0:T(8,128)(2,1)S(1)}, u32[]{:S(2)}, u32[]{:S(2)}) collective-permute-start(bf16[16,32,128]{2,1,0:T(8,128)(2,1)S(1)} %level1_0.1.own_ref), channel_id=1, source_target_pairs={{0,4},{1,5},{2,6},{3,7},{4,0},{5,1},{6,2},{7,3},{8,12},{9,13},{10,... | collective-permute-start | bytes 393224 | tf_op jit(solution)/shard_map/ppermute | solution.py:382
  14.8 0.0 collective-permute-done.1.partner_ref
  14.8 0.4 %level1_1.1.after.state_ref = bf16[16,32,128]{2,1,0:T(8,128)(2,1)S(1)} custom-call(bf16[16,32,128]{2,1,0:T(8,128)(2,1)S(1)} %level0_1.1.after.state_ref, bf16[16,32,128]{2,1,0:T(8,128)(2,1)S(1)} %collective-permute-done.1.partner_ref, bf16[16,128,256]{2,1,0:T(8,128)(2,1)S(1)} %get-tuple-element.15.weight_ref), custom_call_target="tpu_custom_call" | custom-call | flops 33554 | bytes 393 | tf_op jit(solution)/shard_map/level1_1/pallas_call | solution.py:171
  15.3 0.4 %own_term.1 = bf16[16,32,128]{2,1,0:T(8,128)(2,1)S(1)} custom-call(bf16[16,32,128]{2,1,0:T(8,128)(2,1)S(1)} %level1_1.1.after.state_ref, bf16[16,32,128]{2,1,0:T(8,128)(2,1)S(1)} %level1_1.1.after.state_ref, bf16[16,64,128]{2,1,0:T(8,128)(2,1)S(1)} %get-tuple-element.20.refs_0_.own_ref), custom_call_target="tpu_custom_call" | custom-call | flops 16777 | bytes 393 | tf_op jit(solution)/shard_map/own_term/pallas_call | solution.py:195
  15.7 1.5 %collective-permute-start.4 = (bf16[16,32,128]{2,1,0:T(8,128)(2,1)S(1)}, bf16[16,32,128]{2,1,0:T(8,128)(2,1)S(1)}, u32[]{:S(2)}, u32[]{:S(2)}) collective-permute-start(bf16[16,32,128]{2,1,0:T(8,128)(2,1)S(1)} %own_term.1), channel_id=1, source_target_pairs={{0,8},{8,0},{16,24},{24,16},{1,9},{9,1},{17,25},{25,17},{2,10},{10... | collective-permute-start | bytes 393224 | tf_op jit(solution)/shard_map/ppermute | solution.py:382
  17.2 1.9 %collective-permute-start.5 = (bf16[16,32,128]{2,1,0:T(8,128)(2,1)S(1)}, bf16[16,32,128]{2,1,0:T(8,128)(2,1)S(1)}, u32[]{:S(2)}, u32[]{:S(2)}) collective-permute-start(bf16[16,32,128]{2,1,0:T(8,128)(2,1)S(1)} %level1_1.1.after.state_ref), channel_id=1, source_target_pairs={{0,12},{1,13},{2,14},{3,15},{4,8},{5,9},{6,10},{7,11},{8,4},{9,5},... | collective-permute-start | bytes 393224 | tf_op jit(solution)/shard_map/ppermute | solution.py:389
  19.1 0.0 copy-done
  19.1 2.8 %near_roots.1 = (bf16[4,32,64,256]{3,2,1,0:T(8,128)(2,1)S(1)}, bf16[4,32,128]{2,1,0:T(8,128)(2,1)S(1)}, bf16[256,128]{1,0:T(8,128)(2,1)S(1)}) custom-call(bf16[128,64,256]{2,1,0:T(8,128)(2,1)} %root_hbm.1, s32[128]{0:T(128)S(1)} %copy-done, bf16[16,32,128]{2,1,0:T(8,128)(2,1)S(1)} %level1_1.1.after.state_ref), custom_call_target="tpu_custom_call" | custom-call | flops 16 | bytes 8388 | tf_op jit(solution)/shard_map/near_roots/pallas_call | solution.py:279
  21.9 2.7 %collective-permute-done.3.partner_ref = bf16[16,32,128]{2,1,0:T(8,128)(2,1)S(1)} collective-permute-done((bf16[16,32,128]{2,1,0:T(8,128)(2,1)S(1)}, bf16[16,32,128]{2,1,0:T(8,128)(2,1)S(1)}, u32[]{:S(2)}, u32[]{:S(2)}) %collective-permute-start.3) | collective-permute-done | bytes 131104 | tf_op jit(solution)/shard_map/ppermute | solution.py:382
  24.6 0.5 %last_own.1 = (bf16[256,128]{1,0:T(8,128)(2,1)S(1)}, bf16[256,128]{1,0:T(8,128)(2,1)S(1)}) custom-call(bf16[256,128]{1,0:T(8,128)(2,1)S(1)} %get-tuple-element.18.after.refs_2_.refs_3_, bf16[16,32,128]{2,1,0:T(8,128)(2,1)S(1)} %level1_0.1.own_ref, bf16[16,32,128]{2,1,0:T(8,128)(2,1)S(1)} %collective-permute-done.3.partner_ref, ...), custom_call_target="tpu_custom_call" | custom-call | flops 33554 | bytes 393 | tf_op jit(solution)/shard_map/last_own/pallas_call | solution.py:237
  25.1 1.6 %collective-permute-start.7 = (bf16[256,128]{1,0:T(8,128)(2,1)S(1)}, bf16[256,128]{1,0:T(8,128)(2,1)S(1)}, u32[]{:S(2)}, u32[]{:S(2)}) collective-permute-start(bf16[256,128]{1,0:T(8,128)(2,1)S(1)} %get-tuple-element.23), channel_id=1, source_target_pairs={{0,16},{8,24},{16,0},{24,8},{1,17},{9,25},{17,1},{25,9},{2,18},{10... | collective-permute-start | bytes 196616 | tf_op jit(solution)/shard_map/ppermute | solution.py:382
  26.7 0.0 collective-permute-done.4.own_ref
  26.7 0.4 %collective-permute-done.5.partner_ref = bf16[16,32,128]{2,1,0:T(8,128)(2,1)S(1)} collective-permute-done((bf16[16,32,128]{2,1,0:T(8,128)(2,1)S(1)}, bf16[16,32,128]{2,1,0:T(8,128)(2,1)S(1)}, u32[]{:S(2)}, u32[]{:S(2)}) %collective-permute-start.5) | collective-permute-done | bytes 131104 | tf_op jit(solution)/shard_map/ppermute | solution.py:389
  27.1 0.0 collective-permute-done.6.cross_ref
  27.1 0.4 %last_other.1 = (bf16[256,128]{1,0:T(8,128)(2,1)S(1)}, bf16[256,128]{1,0:T(8,128)(2,1)S(1)}) custom-call(bf16[256,128]{1,0:T(8,128)(2,1)S(1)} %get-tuple-element.18.after.refs_2_.refs_3_, bf16[16,32,128]{2,1,0:T(8,128)(2,1)S(1)} %collective-permute-done.4.own_ref, bf16[16,32,128]{2,1,0:T(8,128)(2,1)S(1)} %collective-permute-done.5.partner_ref, ...), custom_call_target="tpu_custom_call" | custom-call | flops 33554 | bytes 393 | tf_op jit(solution)/shard_map/last_other/pallas_call | solution.py:237
  27.5 1.6 %collective-permute-start.8 = (bf16[256,128]{1,0:T(8,128)(2,1)S(1)}, bf16[256,128]{1,0:T(8,128)(2,1)S(1)}, u32[]{:S(2)}, u32[]{:S(2)}) collective-permute-start(bf16[256,128]{1,0:T(8,128)(2,1)S(1)} %get-tuple-element.24), channel_id=1, source_target_pairs={{0,16},{8,24},{16,0},{24,8},{1,17},{9,25},{17,1},{25,9},{2,18},{10... | collective-permute-start | bytes 196616 | tf_op jit(solution)/shard_map/ppermute | solution.py:382
  29.1 0.8 %collective-permute-done.7.refs_5_ = bf16[256,128]{1,0:T(8,128)(2,1)S(1)} collective-permute-done((bf16[256,128]{1,0:T(8,128)(2,1)S(1)}, bf16[256,128]{1,0:T(8,128)(2,1)S(1)}, u32[]{:S(2)}, u32[]{:S(2)}) %collective-permute-start.7) | collective-permute-done | bytes 65568 | tf_op jit(solution)/shard_map/ppermute | solution.py:382
  29.9 1.4 %root.2.refs_0_ = bf16[8,2,256,128]{3,2,1,0:T(8,128)(2,1)S(1)} custom-call(bf16[4,32,64,256]{3,2,1,0:T(8,128)(2,1)S(1)} %get-tuple-element.16.refs_0_.refs_1_, bf16[4,32,128]{2,1,0:T(8,128)(2,1)S(1)} %get-tuple-element.17.refs_1_.refs_2_, bf16[256,128]{1,0:T(8,128)(2,1)S(1)} %get-tuple-element.18.after.refs_2_.refs_3_, ...), custom_call_target="tpu_custom_call" | custom-call | flops 50331 | bytes 3145 | tf_op jit(solution)/shard_map/root/pallas_call | solution.py:357
  31.3 0.5 %collective-permute-done.8.refs_4_ = bf16[256,128]{1,0:T(8,128)(2,1)S(1)} collective-permute-done((bf16[256,128]{1,0:T(8,128)(2,1)S(1)}, bf16[256,128]{1,0:T(8,128)(2,1)S(1)}, u32[]{:S(2)}, u32[]{:S(2)}) %collective-permute-start.8) | collective-permute-done | bytes 65568 | tf_op jit(solution)/shard_map/ppermute | solution.py:382
  31.9 1.6 %root.3 = bf16[8,2,256,128]{3,2,1,0:T(8,128)(2,1)} custom-call(bf16[8,2,256,128]{3,2,1,0:T(8,128)(2,1)S(1)} %root.2.refs_0_, bf16[4,32,64,256]{3,2,1,0:T(8,128)(2,1)S(1)} %get-tuple-element.16.refs_0_.refs_1_, bf16[4,32,128]{2,1,0:T(8,128)(2,1)S(1)} %get-tuple-element.17.refs_1_.refs_2_, bf16[256,128]{1,0:T(8,128)(2,1)S(1)} %get-tuple-element.18.after.refs_2_.refs_3_, ...), custom_call_target="tpu_custom_call" | custom-call | flops 16777 | bytes 1048 | tf_op jit(solution)/shard_map/root/pallas_call | solution.py:357
Async XLA Ops:
  1.9 2.0 %collective-permute-start = (bf16[16,2,32,128]{3,2,1,0:T(8,128)(2,1)S(1)}, bf16[16,2,32,128]{3,2,1,0:T(8,128)(2,1)S(1)}, u32[]{:S(2)}, u32[]{:S(2)}) collective-permute-start(bf16[16,2,32,128]{3,2,1,0:T(8,128)(2,1)S(1)} %leaf.1.after.state_ref), channel_id=1, source_target_pairs={{0,1},{1,0},{2,3},{3,2},{4,5},{5,4},{6,7},{7,6},{8,9},{9,8},{10,11... | collective-permute-start | bytes 786440 | tf_op jit(solution)/shard_map/ppermute | solution.py:382
  4.3 14.8 %copy-start = (s32[128]{0:T(128)S(1)}, s32[128]{0:T(128)}, u32[]{:S(2)}) copy-start(s32[128]{0:T(128)} %order_ref.1) | copy-start | bytes 1540
  4.3 7.1 %collective-permute-start.2 = (bf16[16,32,128]{2,1,0:T(8,128)(2,1)S(1)}, bf16[16,32,128]{2,1,0:T(8,128)(2,1)S(1)}, u32[]{:S(2)}, u32[]{:S(2)}) collective-permute-start(bf16[16,32,128]{2,1,0:T(8,128)(2,1)S(1)} %level0_0.1.state_ref), channel_id=1, source_target_pairs={{0,2},{1,3},{2,0},{3,1},{4,6},{5,7},{6,4},{7,5},{8,10},{9,11},{10,... | collective-permute-start | bytes 393224 | tf_op jit(solution)/shard_map/ppermute | solution.py:382
  7.5 7.4 %collective-permute-start.1 = (bf16[16,32,128]{2,1,0:T(8,128)(2,1)S(1)}, bf16[16,32,128]{2,1,0:T(8,128)(2,1)S(1)}, u32[]{:S(2)}, u32[]{:S(2)}) collective-permute-start(bf16[16,32,128]{2,1,0:T(8,128)(2,1)S(1)} %level0_1.1.after.state_ref), channel_id=1, source_target_pairs={{0,2},{1,3},{2,0},{3,1},{4,6},{5,7},{6,4},{7,5},{8,10},{9,11},{10,... | collective-permute-start | bytes 393224 | tf_op jit(solution)/shard_map/ppermute | solution.py:382
  9.3 17.8 %collective-permute-start.6 = (bf16[16,64,128]{2,1,0:T(8,128)(2,1)S(1)}, bf16[16,64,128]{2,1,0:T(8,128)(2,1)S(1)}, u32[]{:S(2)}, u32[]{:S(2)}) collective-permute-start(bf16[16,64,128]{2,1,0:T(8,128)(2,1)S(1)} %get-tuple-element.19.cross_ref), channel_id=1, source_target_pairs={{0,8},{8,0},{16,24},{24,16},{1,9},{9,1},{17,25},{25,17},{2,10},{10... | collective-permute-start | bytes 786440 | tf_op jit(solution)/shard_map/ppermute | solution.py:382
  11.8 12.8 %collective-permute-start.3 = (bf16[16,32,128]{2,1,0:T(8,128)(2,1)S(1)}, bf16[16,32,128]{2,1,0:T(8,128)(2,1)S(1)}, u32[]{:S(2)}, u32[]{:S(2)}) collective-permute-start(bf16[16,32,128]{2,1,0:T(8,128)(2,1)S(1)} %level1_0.1.own_ref), channel_id=1, source_target_pairs={{0,4},{1,5},{2,6},{3,7},{4,0},{5,1},{6,2},{7,3},{8,12},{9,13},{10,... | collective-permute-start | bytes 393224 | tf_op jit(solution)/shard_map/ppermute | solution.py:382
  15.7 11.0 %collective-permute-start.4 = (bf16[16,32,128]{2,1,0:T(8,128)(2,1)S(1)}, bf16[16,32,128]{2,1,0:T(8,128)(2,1)S(1)}, u32[]{:S(2)}, u32[]{:S(2)}) collective-permute-start(bf16[16,32,128]{2,1,0:T(8,128)(2,1)S(1)} %own_term.1), channel_id=1, source_target_pairs={{0,8},{8,0},{16,24},{24,16},{1,9},{9,1},{17,25},{25,17},{2,10},{10... | collective-permute-start | bytes 393224 | tf_op jit(solution)/shard_map/ppermute | solution.py:382
  17.2 9.9 %collective-permute-start.5 = (bf16[16,32,128]{2,1,0:T(8,128)(2,1)S(1)}, bf16[16,32,128]{2,1,0:T(8,128)(2,1)S(1)}, u32[]{:S(2)}, u32[]{:S(2)}) collective-permute-start(bf16[16,32,128]{2,1,0:T(8,128)(2,1)S(1)} %level1_1.1.after.state_ref), channel_id=1, source_target_pairs={{0,12},{1,13},{2,14},{3,15},{4,8},{5,9},{6,10},{7,11},{8,4},{9,5},... | collective-permute-start | bytes 393224 | tf_op jit(solution)/shard_map/ppermute | solution.py:389
  25.1 4.7 %collective-permute-start.7 = (bf16[256,128]{1,0:T(8,128)(2,1)S(1)}, bf16[256,128]{1,0:T(8,128)(2,1)S(1)}, u32[]{:S(2)}, u32[]{:S(2)}) collective-permute-start(bf16[256,128]{1,0:T(8,128)(2,1)S(1)} %get-tuple-element.23), channel_id=1, source_target_pairs={{0,16},{8,24},{16,0},{24,8},{1,17},{9,25},{17,1},{25,9},{2,18},{10... | collective-permute-start | bytes 196616 | tf_op jit(solution)/shard_map/ppermute | solution.py:382
  27.5 4.3 %collective-permute-start.8 = (bf16[256,128]{1,0:T(8,128)(2,1)S(1)}, bf16[256,128]{1,0:T(8,128)(2,1)S(1)}, u32[]{:S(2)}, u32[]{:S(2)}) collective-permute-start(bf16[256,128]{1,0:T(8,128)(2,1)S(1)} %get-tuple-element.24), channel_id=1, source_target_pairs={{0,16},{8,24},{16,0},{24,8},{1,17},{9,25},{17,1},{25,9},{2,18},{10... | collective-permute-start | bytes 196616 | tf_op jit(solution)/shard_map/ppermute | solution.py:382
where the time goes:
time: 33.7 us; the launch traced here: 33.5 us
  starting transfers between devices  14.9 us (44%)
  Pallas kernels  13.9 us (41%)
  waiting for transfers between devices  4.6 us (14%)
    ppermute x8, starting transfers between devices, swap(): lax.ppermute(array, axis, [(i, i ^ bits) for i in range(lax.axis_size(axi...  13 us
    ppermute x8, waiting for transfers between devices, swap(): lax.ppermute(array, axis, [(i, i ^ bits) for i in range(lax.axis_size(axi...  4.18 us
    pallas_call x2, Pallas kernels, level_weights(): call(functools.partial(factor_kernel, levels, pieces), 'factors', [jax.Sh...  3.17 us
    pallas_call x2, Pallas kernels, spectra_of(): call(functools.partial(root_kernel, group, first, last), 'root', jax.Shap...  3.06 us
    pallas_call x1, Pallas kernels, near_roots(): call(functools.partial(near_kernel, group), 'near_roots', [jax.ShapeDtype...  2.76 us
    ppermute x1, starting transfers between devices, swap_both(): return lax.ppermute(array, ('order', 'lat'), pairs)  1.94 us
    pallas_call x1, Pallas kernels, leaf_states(): call(functools.partial(leaf_kernel, pieces, group), 'leaf', jax.ShapeDtyp...  1.88 us
    pallas_call x4, Pallas kernels, next_states(): call(functools.partial(level_kernel, side), name, jax.ShapeDtypeStruct((p...  1.76 us
  transfers between devices with their start and end apart: 9, of which 5 were waited for; matrix products, arithmetic and copies ran while one was open for 0% of the time, Pallas kernels for 30%

commit v1 on v0

--- a/solution.py
+++ b/solution.py
@@ -159,23 +159,69 @@
     )(level_factors, present, after)
 
 
-def level_kernel(side, state_ref, partner_ref, weight_ref, out_ref):
-    for pair in range(out_ref.shape[0]):
+def level_kernel(side, axis, state_ref, partner_ref, weight_ref, *refs):
+    out_ref = refs[0]
+    me = lax.axis_index(axis) // 2
+    for pair in range(weight_ref.shape[0]):
         at = pair if side is None else (pair, side)
         both = jnp.concatenate([state_ref[at], partner_ref[at]], axis=1)
-        out_ref[pair] = contract(both, weight_ref[pair], ((1,), (1,))).astype(BF16)
-
-
-def next_states(name, state, partner, weights, side=None):
+        result = contract(both, weight_ref[pair], ((1,), (1,))).astype(BF16)
+        if len(refs) == 1:
+            out_ref[pair] = result
+            continue
+        early_ref, groups_ref = refs[1:]
+        owners, group, _ = groups_ref.shape[1:]
+        for owner in range(owners):
+            groups_ref[pair, owner] = result[owner * group : (owner + 1) * group]
+        for k in range(owners):
+            rows = pl.ds((k - 1) % owners * group, group)
+            part = groups_ref[pair, me ^ k]
+            out_ref[pair, rows] = part
+            if k:
+                early_ref[pair, rows] = part
+
+
+def next_states(name, state, partner, weights, side=None, owners=1):
     pairs, rows, lanes = state.shape[0], *state.shape[-2:]
-    return call(
-        functools.partial(level_kernel, side),
+    group = rows // owners
+    split = owners > 1 and group % 16 == 0
+    shapes = [(pairs, rows, lanes)] + [(pairs, rows - group, lanes)] * split
+    outs = call(
+        functools.partial(level_kernel, side, "order"),
         name,
-        jax.ShapeDtypeStruct((pairs, rows, lanes), BF16),
+        [jax.ShapeDtypeStruct(shape, BF16) for shape in shapes],
         whole_blocks(3),
         4 * pairs * rows * lanes * lanes,
         6 * pairs * rows * lanes,
+        [pltpu.VMEM((pairs, owners, group, lanes), BF16)] if split else [],
     )(state, partner, weights)
+    if owners > 1 and not split:
+        me = lax.axis_index("order") // 2
+        parts = [lax.dynamic_slice_in_dim(outs[0], (me ^ k) * group, group, 1) for k in range(owners)]
+        early = jnp.concatenate(parts[1:], axis=1)
+        return [jnp.concatenate([early, parts[0]], axis=1), early]
+    return outs if split else outs[0]
+
+
+def late_kernel(after, state_ref, out_ref):
+    del after
+    rows = out_ref.shape[1]
+    for pair in range(state_ref.shape[0]):
+        out_ref[pair] = state_ref[pair, state_ref.shape[1] - rows :]
+
+
+def late_columns(after, state, rows):
+    pairs, columns, lanes = state.shape
+    if rows % 16:
+        return state[:, columns - rows :]
+    return call(
+        late_kernel,
+        "late_columns",
+        jax.ShapeDtypeStruct((pairs, rows, lanes), BF16),
+        [ANYWHERE] + whole_blocks(1),
+        1,
+        4 * pairs * rows * lanes,
+    )(after, state)
 
 
 def by_slot(packed):
@@ -202,50 +248,54 @@
     )(after, state, own)
 
 
-def last_level_kernel(axis, after, own_ref, partner_ref, cross_ref, *refs):
+def last_level_kernel(turn, begin, axis, after, own_ref, partner_ref, cross_ref, *refs):
     del after
     refs = list(refs)
     own_factor_ref = refs.pop(0) if refs[0].shape == cross_ref.shape else None
     out_refs, groups_ref = refs[:-1], refs[-1]
-    me = lax.axis_index(axis) // 2
+    me = lax.axis_index(axis) // 2 if turn else 0
     pairs, owners, group, _ = groups_ref.shape
     for pair in range(pairs):
         cross = by_slot(cross_ref[pair])
+        own = own_ref[pair, begin : begin + owners * group]
         if own_factor_ref is None:
-            result = own_ref[pair].astype(F32) + contract(partner_ref[pair], cross, ((1,), (1,)))
+            result = own.astype(F32) + contract(partner_ref[pair], cross, ((1,), (1,)))
         else:
             weight = jnp.concatenate([by_slot(own_factor_ref[pair]), cross], axis=1)
-            both = jnp.concatenate([own_ref[pair], partner_ref[pair]], axis=1)
+            both = jnp.concatenate([own, partner_ref[pair]], axis=1)
             result = contract(both, weight, ((1,), (1,)))
         result = result.astype(BF16)
-        if len(out_refs) == 1:
+        if group % 16:
             out_refs[0][pair] = result
             continue
         for owner in range(owners):
             groups_ref[pair, owner] = result[owner * group : (owner + 1) * group]
-    if len(out_refs) > 1:
+    if group % 16 == 0:
         for k, out_ref in enumerate(out_refs):
             for pair in range(pairs):
                 out_ref[pl.ds(pair * group, group)] = groups_ref[pair, me ^ k]
 
 
-def last_states(name, after, own, partner, factors, owners):
-    pairs, columns, lanes = own.shape
+def last_states(name, after, own, partner, factors, owners, turn, begin=0):
+    pairs, columns, lanes = partner.shape
     group = columns // owners
     rows = pairs * group
-    by_owner = group % 16 == 0 and owners > 1
+    aligned = group % 16 == 0
+    if not aligned:
+        own = own[:, begin : begin + columns]
+        begin = 0
     parts = call(
-        functools.partial(last_level_kernel, "order"),
+        functools.partial(last_level_kernel, turn, begin, "order"),
         name,
-        [jax.ShapeDtypeStruct((rows, lanes), BF16)] * owners if by_owner else [jax.ShapeDtypeStruct(own.shape, BF16)],
+        [jax.ShapeDtypeStruct((rows, lanes), BF16)] * owners if aligned else [jax.ShapeDtypeStruct(own.shape, BF16)],
         [ANYWHERE] + whole_blocks(2 + len(factors)),
         4 * pairs * columns * lanes * lanes,
         6 * pairs * columns * lanes,
         [pltpu.VMEM((pairs, owners, group, lanes), BF16)],
     )(after, own, partner, *factors)
-    if by_owner:
+    if aligned:
         return parts
-    me = lax.axis_index("order") // 2
+    me = lax.axis_index("order") // 2 if turn else 0
     parts = [lax.dynamic_slice_in_dim(parts[0], (me ^ k) * group, group, 1) for k in range(owners)]
     return [part.reshape(rows, lanes) for part in parts]
 
@@ -395,19 +445,27 @@
     weights += level_weights(level_factors, present, tuple(range(1, levels)), states[1])
     own_factors, cross_factors = weights[-2:]
     other_cross = swap(cross_factors, "order", 1)
+    high = owners // 2
+    own_columns = columns // owners
     for level in range(1, levels - 1):
         partners = [swap(state, "lat", 1 << level) for state in states]
-        states = [next_states(f"level{level}_{c}", states[c], partners[c], weights[level]) for c in range(2)]
+        parts = high if level == levels - 2 else 1
+        states = [
+            next_states(f"level{level}_{c}", states[c], partners[c], weights[level], None, parts if c else 1)
+            for c in range(2)
+        ]
     top = 1 << levels - 1
-    partner = swap(states[0], "lat", top)
-    other_partner = swap_both(states[1], 1, top)
-    other_own = swap(own_term(states[1], states[1], own_factors), "order", 1)
-    roots, places, alive = near_roots(root_basis, order_of_slot, owners, group, states[1])
-    both = (
-        last_states("last_own", alive, states[0], partner, (cross_factors, own_factors), owners // 2),
-        last_states("last_other", alive, other_own, other_partner, (other_cross,), owners // 2),
-    )
-    arrived = [swap(both[k % 2][k // 2], "order", k // 2 * 2) if k > 1 else both[k][0] for k in range(owners)]
+    mine, (other, early) = states
+    mine_partner = swap(mine, "lat", top)
+    early_partner = swap_both(early, 1, top)
+    other_own = swap(own_term(other, other, own_factors), "order", 1)
+    roots, places, alive = near_roots(root_basis, order_of_slot, owners, group, other)
+    late_partner = swap_both(late_columns(alive, other, own_columns), 1, top)
+    even = last_states("last_own", alive, mine, mine_partner, (cross_factors, own_factors), high, True)
+    begin = columns // 2 - own_columns
+    odd = last_states("last_early", alive, other_own, early_partner, (other_cross,), high - 1, False)
+    odd = [*last_states("last_late", alive, other_own, late_partner, (other_cross,), 1, False, begin), *odd]
+    arrived = [swap((odd if k % 2 else even)[k // 2], "order", k // 2 * 2) if k > 1 else (even, odd)[k][0] for k in range(owners)]
     early = 3 * owners // 4
     spectra = spectra_of(arrived[:early], roots, places, alive, None, 0, group)
     return spectra_of(arrived[early:], roots, places, alive, spectra, early, group)

time: 33.7 us -> 32.5 us (0.964)
  waiting for transfers between devices: 4.6 us -> 2.07 us
  starting transfers between devices: 14.9 us -> 15.8 us
  Pallas kernels: 13.9 us -> 14.3 us
    ppermute x8, waiting for transfers between devices: 4.18 us -> 0.9 us  [swap(): lax.ppermute(array, axis, [(i, i ^ bits) for i in range(lax.axis_size(axi...]
    ppermute x1 -> x2, starting transfers between devices: 1.94 us -> 3.89 us  [swap_both(): return lax.ppermute(array, ('order', 'lat'), pairs)]
    ppermute x8, starting transfers between devices: 13 us -> 12 us  [swap(): lax.ppermute(array, axis, [(i, i ^ bits) for i in range(lax.axis_size(axi...]
    ppermute x1 -> x2, waiting for transfers between devices: 0.42 us -> 1.17 us  [swap_both(): return lax.ppermute(array, ('order', 'lat'), pairs)]
    pallas_call x6 -> x8, Pallas kernels: 2.63 us -> 3.02 us  [the longest x4 1.79 us: next_states(): call(functools.partial(level_kernel, side, 'order'), name, [jax.ShapeDtyp...]
  transfers between devices with their start and end apart: 9 -> 10, of which waited for: 5 -> 4; matrix products, arithmetic and copies ran while one was open for 0% -> 0% of each run, Pallas kernels for 30% -> 32%
where the time goes in v1:
time: 32.5 us; the launch traced here: 32.3 us
  starting transfers between devices  15.8 us (49%)
  Pallas kernels  14.3 us (44%)
  waiting for transfers between devices  2.07 us (6%)
    ppermute x8, starting transfers between devices, swap(): lax.ppermute(array, axis, [(i, i ^ bits) for i in range(lax.axis_size(axi...  12 us
    ppermute x2, starting transfers between devices, swap_both(): return lax.ppermute(array, ('order', 'lat'), pairs)  3.89 us
    pallas_call x2, Pallas kernels, level_weights(): call(functools.partial(factor_kernel, levels, pieces), 'factors', [jax.Sh...  3.17 us
    pallas_call x2, Pallas kernels, spectra_of(): call(functools.partial(root_kernel, group, first, last), 'root', jax.Shap...  3.05 us
    pallas_call x1, Pallas kernels, near_roots(): call(functools.partial(near_kernel, group), 'near_roots', [jax.ShapeDtype...  2.76 us
    pallas_call x1, Pallas kernels, leaf_states(): call(functools.partial(leaf_kernel, pieces, group), 'leaf', jax.ShapeDtyp...  1.88 us
    pallas_call x4, Pallas kernels, next_states(): call(functools.partial(level_kernel, side, 'order'), name, [jax.ShapeDtyp...  1.79 us
    pallas_call x3, Pallas kernels, last_states(): call(functools.partial(last_level_kernel, turn, begin, 'order'), name, [j...  1.23 us
  transfers between devices with their start and end apart: 10, of which 4 were waited for; matrix products, arithmetic and copies ran while one was open for 0% of the time, Pallas kernels for 32%

profile of v1, /device:TPU:0, one launch (start us, length us, event | category | flops | bytes accessed | tf_op | source)
XLA Modules:
  0.0 32.3 jit_solution(3353467377462957574)
XLA Ops:
  0.0 1.9 %leaf.1.after.state_ref = bf16[16,2,32,128]{3,2,1,0:T(8,128)(2,1)S(1)} custom-call(bf16[32,64,256]{2,1,0:T(8,128)(2,1)} %fourier_hbm.1, f32[1,256]{1,0:T(1,128)} %bitcast.4, bf16[32,64,256]{2,1,0:T(8,128)(2,1)} %leaf_hbm.1), custom_call_target="tpu_custom_call" | custom-call | flops 67108 | bytes 2097 | tf_op jit(solution)/shard_map/leaf/pallas_call | solution.py:83
  1.9 0.5 %collective-permute-start = (bf16[16,2,32,128]{3,2,1,0:T(8,128)(2,1)S(1)}, bf16[16,2,32,128]{3,2,1,0:T(8,128)(2,1)S(1)}, u32[]{:S(2)}, u32[]{:S(2)}) collective-permute-start(bf16[16,2,32,128]{3,2,1,0:T(8,128)(2,1)S(1)} %leaf.1.after.state_ref), channel_id=1, source_target_pairs={{0,1},{1,0},{2,3},{3,2},{4,5},{5,4},{6,7},{7,6},{8,9},{9,8},{10,11... | collective-permute-start | bytes 786440 | tf_op jit(solution)/shard_map/ppermute | solution.py:432
  2.4 1.4 %factors.2.weight_ref = bf16[16,128,256]{2,1,0:T(8,128)(2,1)S(1)} custom-call(bf16[32,3,2,1,64,64]{5,4,3,2,1,0:T(8,128)(2,1)} %factor_hbm.3, s32[3,1,32]{2,1,0:T(1,128)} %bitcast.2, bf16[16,2,32,128]{3,2,1,0:T(8,128)(2,1)S(1)} %leaf.1.after.state_ref), custom_call_target="tpu_custom_call" | custom-call | flops 524 | bytes 2097 | tf_op jit(solution)/shard_map/factors/pallas_call | solution.py:142
  3.9 0.0 collective-permute-done.partner_ref
  3.9 0.4 %level0_0.1.state_ref = bf16[16,32,128]{2,1,0:T(8,128)(2,1)S(1)} custom-call(bf16[16,2,32,128]{3,2,1,0:T(8,128)(2,1)S(1)} %leaf.1.after.state_ref, bf16[16,2,32,128]{3,2,1,0:T(8,128)(2,1)S(1)} %collective-permute-done.partner_ref, bf16[16,128,256]{2,1,0:T(8,128)(2,1)S(1)} %factors.2.weight_ref), custom_call_target="tpu_custom_call" | custom-call | flops 33554 | bytes 393 | tf_op jit(solution)/shard_map/level0_0/pallas_call | solution.py:189
  4.3 0.0 copy-start
  4.3 2.7 %collective-permute-start.2 = (bf16[16,32,128]{2,1,0:T(8,128)(2,1)S(1)}, bf16[16,32,128]{2,1,0:T(8,128)(2,1)S(1)}, u32[]{:S(2)}, u32[]{:S(2)}) collective-permute-start(bf16[16,32,128]{2,1,0:T(8,128)(2,1)S(1)} %level0_0.1.state_ref), channel_id=1, source_target_pairs={{0,2},{1,3},{2,0},{3,1},{4,6},{5,7},{6,4},{7,5},{8,10},{9,11},{10,... | collective-permute-start | bytes 393224 | tf_op jit(solution)/shard_map/ppermute | solution.py:432
  7.0 0.4 %level0_1.1.after.state_ref = bf16[16,32,128]{2,1,0:T(8,128)(2,1)S(1)} custom-call(bf16[16,2,32,128]{3,2,1,0:T(8,128)(2,1)S(1)} %leaf.1.after.state_ref, bf16[16,2,32,128]{3,2,1,0:T(8,128)(2,1)S(1)} %collective-permute-done.partner_ref, bf16[16,128,256]{2,1,0:T(8,128)(2,1)S(1)} %factors.2.weight_ref), custom_call_target="tpu_custom_call" | custom-call | flops 33554 | bytes 393 | tf_op jit(solution)/shard_map/level0_1/pallas_call | solution.py:189
  7.5 0.1 collective-permute-start.1
  7.5 1.7 %factors.3 = (bf16[16,128,256]{2,1,0:T(8,128)(2,1)S(1)}, bf16[16,64,128]{2,1,0:T(8,128)(2,1)S(1)}, bf16[16,64,128]{2,1,0:T(8,128)(2,1)S(1)}) custom-call(bf16[32,3,2,1,64,64]{5,4,3,2,1,0:T(8,128)(2,1)} %factor_hbm.3, s32[3,1,32]{2,1,0:T(1,128)} %bitcast.3, bf16[16,32,128]{2,1,0:T(8,128)(2,1)S(1)} %level0_1.1.after.state_ref), custom_call_target="tpu_custom_call" | custom-call | flops 1048 | bytes 4194 | tf_op jit(solution)/shard_map/factors/pallas_call | solution.py:142
  9.3 2.0 %collective-permute-start.6 = (bf16[16,64,128]{2,1,0:T(8,128)(2,1)S(1)}, bf16[16,64,128]{2,1,0:T(8,128)(2,1)S(1)}, u32[]{:S(2)}, u32[]{:S(2)}) collective-permute-start(bf16[16,64,128]{2,1,0:T(8,128)(2,1)S(1)} %get-tuple-element.20.cross_ref), channel_id=1, source_target_pairs={{0,8},{8,0},{16,24},{24,16},{1,9},{9,1},{17,25},{25,17},{2,10},{10... | collective-permute-start | bytes 786440 | tf_op jit(solution)/shard_map/ppermute | solution.py:432
  11.3 0.1 collective-permute-done.2.partner_ref
  11.4 0.4 %level1_0.1.own_ref = bf16[16,32,128]{2,1,0:T(8,128)(2,1)S(1)} custom-call(bf16[16,32,128]{2,1,0:T(8,128)(2,1)S(1)} %level0_0.1.state_ref, bf16[16,32,128]{2,1,0:T(8,128)(2,1)S(1)} %collective-permute-done.2.partner_ref, bf16[16,128,256]{2,1,0:T(8,128)(2,1)S(1)} %get-tuple-element.15.weight_ref), custom_call_target="tpu_custom_call" | custom-call | flops 33554 | bytes 393 | tf_op jit(solution)/shard_map/level1_0/pallas_call | solution.py:189
  11.8 3.0 %collective-permute-start.3 = (bf16[16,32,128]{2,1,0:T(8,128)(2,1)S(1)}, bf16[16,32,128]{2,1,0:T(8,128)(2,1)S(1)}, u32[]{:S(2)}, u32[]{:S(2)}) collective-permute-start(bf16[16,32,128]{2,1,0:T(8,128)(2,1)S(1)} %level1_0.1.own_ref), channel_id=1, source_target_pairs={{0,4},{1,5},{2,6},{3,7},{4,0},{5,1},{6,2},{7,3},{8,12},{9,13},{10,... | collective-permute-start | bytes 393224 | tf_op jit(solution)/shard_map/ppermute | solution.py:432
  14.8 0.0 collective-permute-done.1.partner_ref
  14.8 0.5 %level1_1.1 = (bf16[16,32,128]{2,1,0:T(8,128)(2,1)S(1)}, bf16[16,16,128]{2,1,0:T(8,128)(2,1)S(1)}) custom-call(bf16[16,32,128]{2,1,0:T(8,128)(2,1)S(1)} %level0_1.1.after.state_ref, bf16[16,32,128]{2,1,0:T(8,128)(2,1)S(1)} %collective-permute-done.1.partner_ref, bf16[16,128,256]{2,1,0:T(8,128)(2,1)S(1)} %get-tuple-element.15.weight_ref), custom_call_target="tpu_custom_call" | custom-call | flops 33554 | bytes 393 | tf_op jit(solution)/shard_map/level1_1/pallas_call | solution.py:189
  15.3 0.4 %own_term.1 = bf16[16,32,128]{2,1,0:T(8,128)(2,1)S(1)} custom-call(bf16[16,32,128]{2,1,0:T(8,128)(2,1)S(1)} %get-tuple-element.16.after.state_ref, bf16[16,32,128]{2,1,0:T(8,128)(2,1)S(1)} %get-tuple-element.16.after.state_ref, bf16[16,64,128]{2,1,0:T(8,128)(2,1)S(1)} %get-tuple-element.21.refs_0_.own_ref), custom_call_target="tpu_custom_call" | custom-call | flops 16777 | bytes 393 | tf_op jit(solution)/shard_map/own_term/pallas_call | solution.py:241
  15.7 1.5 %collective-permute-start.4 = (bf16[16,32,128]{2,1,0:T(8,128)(2,1)S(1)}, bf16[16,32,128]{2,1,0:T(8,128)(2,1)S(1)}, u32[]{:S(2)}, u32[]{:S(2)}) collective-permute-start(bf16[16,32,128]{2,1,0:T(8,128)(2,1)S(1)} %own_term.1), channel_id=1, source_target_pairs={{0,8},{8,0},{16,24},{24,16},{1,9},{9,1},{17,25},{25,17},{2,10},{10... | collective-permute-start | bytes 393224 | tf_op jit(solution)/shard_map/ppermute | solution.py:432
  17.2 1.9 %collective-permute-start.8 = (bf16[16,16,128]{2,1,0:T(8,128)(2,1)S(1)}, bf16[16,16,128]{2,1,0:T(8,128)(2,1)S(1)}, u32[]{:S(2)}, u32[]{:S(2)}) collective-permute-start(bf16[16,16,128]{2,1,0:T(8,128)(2,1)S(1)} %get-tuple-element.24), channel_id=1, source_target_pairs={{0,12},{1,13},{2,14},{3,15},{4,8},{5,9},{6,10},{7,11},{8,4},{9,5},... | collective-permute-start | bytes 196616 | tf_op jit(solution)/shard_map/ppermute | solution.py:439
  19.2 0.0 copy-done
  19.2 2.8 %near_roots.1 = (bf16[4,32,64,256]{3,2,1,0:T(8,128)(2,1)S(1)}, bf16[4,32,128]{2,1,0:T(8,128)(2,1)S(1)}, bf16[256,128]{1,0:T(8,128)(2,1)S(1)}) custom-call(bf16[128,64,256]{2,1,0:T(8,128)(2,1)} %root_hbm.1, s32[128]{0:T(128)S(1)} %copy-done, bf16[16,32,128]{2,1,0:T(8,128)(2,1)S(1)} %get-tuple-element.16.after.state_ref), custom_call_target="tpu_custom_call" | custom-call | flops 16 | bytes 8388 | tf_op jit(solution)/shard_map/near_roots/pallas_call | solution.py:329
  21.9 2.0 %collective-permute-start.5 = (bf16[16,16,128]{2,1,0:T(8,128)(2,1)S(1)}, bf16[16,16,128]{2,1,0:T(8,128)(2,1)S(1)}, u32[]{:S(2)}, u32[]{:S(2)}) collective-permute-start(bf16[16,16,128]{2,1,0:T(8,128)(2,1)S(1)} %late_columns.1), channel_id=1, source_target_pairs={{0,12},{1,13},{2,14},{3,15},{4,8},{5,9},{6,10},{7,11},{8,4},{9,5},... | collective-permute-start | bytes 196616 | tf_op jit(solution)/shard_map/ppermute | solution.py:439
  23.9 0.0 collective-permute-done.3.partner_ref
  23.9 0.5 %last_own.1 = (bf16[256,128]{1,0:T(8,128)(2,1)S(1)}, bf16[256,128]{1,0:T(8,128)(2,1)S(1)}) custom-call(bf16[256,128]{1,0:T(8,128)(2,1)S(1)} %get-tuple-element.19.after.refs_2_.refs_3_, bf16[16,32,128]{2,1,0:T(8,128)(2,1)S(1)} %level1_0.1.own_ref, bf16[16,32,128]{2,1,0:T(8,128)(2,1)S(1)} %collective-permute-done.3.partner_ref, ...), custom_call_target="tpu_custom_call" | custom-call | flops 33554 | bytes 393 | tf_op jit(solution)/shard_map/last_own/pallas_call | solution.py:287
  24.4 1.6 %collective-permute-start.7 = (bf16[256,128]{1,0:T(8,128)(2,1)S(1)}, bf16[256,128]{1,0:T(8,128)(2,1)S(1)}, u32[]{:S(2)}, u32[]{:S(2)}) collective-permute-start(bf16[256,128]{1,0:T(8,128)(2,1)S(1)} %get-tuple-element.23), channel_id=1, source_target_pairs={{0,16},{8,24},{16,0},{24,8},{1,17},{9,25},{17,1},{25,9},{2,18},{10... | collective-permute-start | bytes 196616 | tf_op jit(solution)/shard_map/ppermute | solution.py:432
  26.0 0.0 collective-permute-done.8.partner_ref
  26.0 0.0 collective-permute-done.4.own_ref
  26.0 0.0 collective-permute-done.6.cross_ref
  26.0 0.4 %last_early.1 = bf16[256,128]{1,0:T(8,128)(2,1)S(1)} custom-call(bf16[256,128]{1,0:T(8,128)(2,1)S(1)} %get-tuple-element.19.after.refs_2_.refs_3_, bf16[16,32,128]{2,1,0:T(8,128)(2,1)S(1)} %collective-permute-done.4.own_ref, bf16[16,16,128]{2,1,0:T(8,128)(2,1)S(1)} %collective-permute-done.8.partner_ref, ...), custom_call_target="tpu_custom_call" | custom-call | flops 16777 | bytes 196 | tf_op jit(solution)/shard_map/last_early/pallas_call | solution.py:287
  26.4 0.5 %collective-permute-start.9 = (bf16[256,128]{1,0:T(8,128)(2,1)S(1)}, bf16[256,128]{1,0:T(8,128)(2,1)S(1)}, u32[]{:S(2)}, u32[]{:S(2)}) collective-permute-start(bf16[256,128]{1,0:T(8,128)(2,1)S(1)} %last_early.1), channel_id=1, source_target_pairs={{0,16},{8,24},{16,0},{24,8},{1,17},{9,25},{17,1},{25,9},{2,18},{10... | collective-permute-start | bytes 196616 | tf_op jit(solution)/shard_map/ppermute | solution.py:432
  26.9 1.2 %collective-permute-done.5.partner_ref = bf16[16,16,128]{2,1,0:T(8,128)(2,1)S(1)} collective-permute-done((bf16[16,16,128]{2,1,0:T(8,128)(2,1)S(1)}, bf16[16,16,128]{2,1,0:T(8,128)(2,1)S(1)}, u32[]{:S(2)}, u32[]{:S(2)}) %collective-permute-start.5) | collective-permute-done | bytes 65568 | tf_op jit(solution)/shard_map/ppermute | solution.py:439
  28.1 0.4 %last_late.1.refs_4_ = bf16[256,128]{1,0:T(8,128)(2,1)S(1)} custom-call(bf16[256,128]{1,0:T(8,128)(2,1)S(1)} %get-tuple-element.19.after.refs_2_.refs_3_, bf16[16,32,128]{2,1,0:T(8,128)(2,1)S(1)} %collective-permute-done.4.own_ref, bf16[16,16,128]{2,1,0:T(8,128)(2,1)S(1)} %collective-permute-done.5.partner_ref, ...), custom_call_target="tpu_custom_call" | custom-call | flops 16777 | bytes 196 | tf_op jit(solution)/shard_map/last_late/pallas_call | solution.py:287
  28.4 0.3 collective-permute-done.7.refs_5_
  28.7 1.4 %root.2.refs_0_ = bf16[8,2,256,128]{3,2,1,0:T(8,128)(2,1)S(1)} custom-call(bf16[4,32,64,256]{3,2,1,0:T(8,128)(2,1)S(1)} %get-tuple-element.17.refs_0_.refs_1_, bf16[4,32,128]{2,1,0:T(8,128)(2,1)S(1)} %get-tuple-element.18.refs_1_.refs_2_, bf16[256,128]{1,0:T(8,128)(2,1)S(1)} %get-tuple-element.19.after.refs_2_.refs_3_, ...), custom_call_target="tpu_custom_call" | custom-call | flops 50331 | bytes 3145 | tf_op jit(solution)/shard_map/root/pallas_call | solution.py:407
  30.1 0.5 %collective-permute-done.9.refs_4_ = bf16[256,128]{1,0:T(8,128)(2,1)S(1)} collective-permute-done((bf16[256,128]{1,0:T(8,128)(2,1)S(1)}, bf16[256,128]{1,0:T(8,128)(2,1)S(1)}, u32[]{:S(2)}, u32[]{:S(2)}) %collective-permute-start.9) | collective-permute-done | bytes 65568 | tf_op jit(solution)/shard_map/ppermute | solution.py:432
  30.7 1.6 %root.3 = bf16[8,2,256,128]{3,2,1,0:T(8,128)(2,1)} custom-call(bf16[8,2,256,128]{3,2,1,0:T(8,128)(2,1)S(1)} %root.2.refs_0_, bf16[4,32,64,256]{3,2,1,0:T(8,128)(2,1)S(1)} %get-tuple-element.17.refs_0_.refs_1_, bf16[4,32,128]{2,1,0:T(8,128)(2,1)S(1)} %get-tuple-element.18.refs_1_.refs_2_, bf16[256,128]{1,0:T(8,128)(2,1)S(1)} %get-tuple-element.19.after.refs_2_.refs_3_, ...), custom_call_target="tpu_custom_call" | custom-call | flops 16777 | bytes 1048 | tf_op jit(solution)/shard_map/root/pallas_call | solution.py:407
  (1 shorter events, 0.0 us)
Async XLA Ops:
  1.9 2.0 %collective-permute-start = (bf16[16,2,32,128]{3,2,1,0:T(8,128)(2,1)S(1)}, bf16[16,2,32,128]{3,2,1,0:T(8,128)(2,1)S(1)}, u32[]{:S(2)}, u32[]{:S(2)}) collective-permute-start(bf16[16,2,32,128]{3,2,1,0:T(8,128)(2,1)S(1)} %leaf.1.after.state_ref), channel_id=1, source_target_pairs={{0,1},{1,0},{2,3},{3,2},{4,5},{5,4},{6,7},{7,6},{8,9},{9,8},{10,11... | collective-permute-start | bytes 786440 | tf_op jit(solution)/shard_map/ppermute | solution.py:432
  4.3 14.9 %copy-start = (s32[128]{0:T(128)S(1)}, s32[128]{0:T(128)}, u32[]{:S(2)}) copy-start(s32[128]{0:T(128)} %order_ref.1) | copy-start | bytes 1540
  4.3 7.1 %collective-permute-start.2 = (bf16[16,32,128]{2,1,0:T(8,128)(2,1)S(1)}, bf16[16,32,128]{2,1,0:T(8,128)(2,1)S(1)}, u32[]{:S(2)}, u32[]{:S(2)}) collective-permute-start(bf16[16,32,128]{2,1,0:T(8,128)(2,1)S(1)} %level0_0.1.state_ref), channel_id=1, source_target_pairs={{0,2},{1,3},{2,0},{3,1},{4,6},{5,7},{6,4},{7,5},{8,10},{9,11},{10,... | collective-permute-start | bytes 393224 | tf_op jit(solution)/shard_map/ppermute | solution.py:432
  7.5 7.4 %collective-permute-start.1 = (bf16[16,32,128]{2,1,0:T(8,128)(2,1)S(1)}, bf16[16,32,128]{2,1,0:T(8,128)(2,1)S(1)}, u32[]{:S(2)}, u32[]{:S(2)}) collective-permute-start(bf16[16,32,128]{2,1,0:T(8,128)(2,1)S(1)} %level0_1.1.after.state_ref), channel_id=1, source_target_pairs={{0,2},{1,3},{2,0},{3,1},{4,6},{5,7},{6,4},{7,5},{8,10},{9,11},{10,... | collective-permute-start | bytes 393224 | tf_op jit(solution)/shard_map/ppermute | solution.py:432
  9.3 16.7 %collective-permute-start.6 = (bf16[16,64,128]{2,1,0:T(8,128)(2,1)S(1)}, bf16[16,64,128]{2,1,0:T(8,128)(2,1)S(1)}, u32[]{:S(2)}, u32[]{:S(2)}) collective-permute-start(bf16[16,64,128]{2,1,0:T(8,128)(2,1)S(1)} %get-tuple-element.20.cross_ref), channel_id=1, source_target_pairs={{0,8},{8,0},{16,24},{24,16},{1,9},{9,1},{17,25},{25,17},{2,10},{10... | collective-permute-start | bytes 786440 | tf_op jit(solution)/shard_map/ppermute | solution.py:432
  11.8 12.1 %collective-permute-start.3 = (bf16[16,32,128]{2,1,0:T(8,128)(2,1)S(1)}, bf16[16,32,128]{2,1,0:T(8,128)(2,1)S(1)}, u32[]{:S(2)}, u32[]{:S(2)}) collective-permute-start(bf16[16,32,128]{2,1,0:T(8,128)(2,1)S(1)} %level1_0.1.own_ref), channel_id=1, source_target_pairs={{0,4},{1,5},{2,6},{3,7},{4,0},{5,1},{6,2},{7,3},{8,12},{9,13},{10,... | collective-permute-start | bytes 393224 | tf_op jit(solution)/shard_map/ppermute | solution.py:432
  15.7 10.3 %collective-permute-start.4 = (bf16[16,32,128]{2,1,0:T(8,128)(2,1)S(1)}, bf16[16,32,128]{2,1,0:T(8,128)(2,1)S(1)}, u32[]{:S(2)}, u32[]{:S(2)}) collective-permute-start(bf16[16,32,128]{2,1,0:T(8,128)(2,1)S(1)} %own_term.1), channel_id=1, source_target_pairs={{0,8},{8,0},{16,24},{24,16},{1,9},{9,1},{17,25},{25,17},{2,10},{10... | collective-permute-start | bytes 393224 | tf_op jit(solution)/shard_map/ppermute | solution.py:432
  17.2 8.7 %collective-permute-start.8 = (bf16[16,16,128]{2,1,0:T(8,128)(2,1)S(1)}, bf16[16,16,128]{2,1,0:T(8,128)(2,1)S(1)}, u32[]{:S(2)}, u32[]{:S(2)}) collective-permute-start(bf16[16,16,128]{2,1,0:T(8,128)(2,1)S(1)} %get-tuple-element.24), channel_id=1, source_target_pairs={{0,12},{1,13},{2,14},{3,15},{4,8},{5,9},{6,10},{7,11},{8,4},{9,5},... | collective-permute-start | bytes 196616 | tf_op jit(solution)/shard_map/ppermute | solution.py:439
  21.9 6.1 %collective-permute-start.5 = (bf16[16,16,128]{2,1,0:T(8,128)(2,1)S(1)}, bf16[16,16,128]{2,1,0:T(8,128)(2,1)S(1)}, u32[]{:S(2)}, u32[]{:S(2)}) collective-permute-start(bf16[16,16,128]{2,1,0:T(8,128)(2,1)S(1)} %late_columns.1), channel_id=1, source_target_pairs={{0,12},{1,13},{2,14},{3,15},{4,8},{5,9},{6,10},{7,11},{8,4},{9,5},... | collective-permute-start | bytes 196616 | tf_op jit(solution)/shard_map/ppermute | solution.py:439
  24.4 4.3 %collective-permute-start.7 = (bf16[256,128]{1,0:T(8,128)(2,1)S(1)}, bf16[256,128]{1,0:T(8,128)(2,1)S(1)}, u32[]{:S(2)}, u32[]{:S(2)}) collective-permute-start(bf16[256,128]{1,0:T(8,128)(2,1)S(1)} %get-tuple-element.23), channel_id=1, source_target_pairs={{0,16},{8,24},{16,0},{24,8},{1,17},{9,25},{17,1},{25,9},{2,18},{10... | collective-permute-start | bytes 196616 | tf_op jit(solution)/shard_map/ppermute | solution.py:432
  26.4 4.3 %collective-permute-start.9 = (bf16[256,128]{1,0:T(8,128)(2,1)S(1)}, bf16[256,128]{1,0:T(8,128)(2,1)S(1)}, u32[]{:S(2)}, u32[]{:S(2)}) collective-permute-start(bf16[256,128]{1,0:T(8,128)(2,1)S(1)} %last_early.1), channel_id=1, source_target_pairs={{0,16},{8,24},{16,0},{24,8},{1,17},{9,25},{17,1},{25,9},{2,18},{10... | collective-permute-start | bytes 196616 | tf_op jit(solution)/shard_map/ppermute | solution.py:432
